TPU v7x, 32 devices: a whole 2x2x4 slice. The times are simulated.
32 devices in a mesh: fsdp: 4 (over z), ctx: 4 (over y, x), tp: 2 (over core).
Axes of the slice: x: 2, y: 2, z: 4, core: 2. Of those that a mesh axis runs over, the one named last changes fastest.
Arguments:
- hidden_in: bfloat16 [32768, 768], P(('fsdp', 'ctx')), may hold values from -6 to 6
- cotangent: bfloat16 [32768, 768], P(('fsdp', 'ctx')), may hold values from -6 to 6
- positions: int32 [32768], P(('fsdp', 'ctx')), may hold values from -1 to 8191, as said below
- norm_gain: bfloat16 [768], P(('fsdp', 'ctx')), may hold values from 0.5 to 1.5
- proj_z: bfloat16 [768, 1536], P(('fsdp', 'ctx'), 'tp'), may hold values from -0.21875 to 0.21875
- proj_x: bfloat16 [768, 1536], P(('fsdp', 'ctx'), 'tp'), may hold values from -0.21875 to 0.21875
- proj_bc: bfloat16 [768, 256], P(('fsdp', 'ctx')), may hold values from -0.21875 to 0.21875
- proj_dt: bfloat16 [768, 24], P(('fsdp', 'ctx'), 'tp'), may hold values from -0.21875 to 0.21875
- conv_inner: float32 [4, 1536], P(None, 'tp'), may hold values from -3 to 3
- conv_inner_bias: float32 [1536], P('tp'), may hold values from -0.5 to 0.5
- conv_state: float32 [4, 256], replicated, may hold values from -3 to 3
- conv_state_bias: float32 [256], replicated, may hold values from -0.5 to 0.5
- dt_bias: float32 [24], P('tp'), as said below
- a_log: float32 [24], P('tp'), may hold values from 0 to 2.77
- skip_gain: float32 [24], P('tp'), may hold values from 0.5 to 1.5
- gated_gain: float32 [1536], P('tp'), may hold values from 0.5 to 1.5
- proj_out: bfloat16 [1536, 768], P('tp', ('fsdp', 'ctx')), may hold values from -0.15625 to 0.15625
Outputs:
- hidden_out: bfloat16 [32768, 768], P(('fsdp', 'ctx'))
- grad_hidden: float32 [32768, 768], P(('fsdp', 'ctx'))
- grad_norm_gain: float32 [768], P(('fsdp', 'ctx'))
- grad_proj_z: float32 [768, 1536], P(('fsdp', 'ctx'), 'tp')
- grad_proj_x: float32 [768, 1536], P(('fsdp', 'ctx'), 'tp')
- grad_proj_bc: float32 [768, 256], P(('fsdp', 'ctx'))
- grad_proj_dt: float32 [768, 24], P(('fsdp', 'ctx'), 'tp')
- grad_conv_inner: float32 [4, 1536], P(None, 'tp')
- grad_conv_inner_bias: float32 [1536], P('tp')
- grad_conv_state: float32 [4, 256], replicated
- grad_conv_state_bias: float32 [256], replicated
- grad_dt_bias: float32 [24], P('tp')
- grad_a_log: float32 [24], P('tp')
- grad_skip_gain: float32 [24], P('tp')
- grad_gated_gain: float32 [1536], P('tp')
- grad_proj_out: float32 [1536, 768], P('tp', ('fsdp', 'ctx'))
Inputs may be any that keep to these rules, and one draw needn't show every extreme that they name: `positions`: each group of 8192 consecutive rows (one index of fsdp) begins with a sequence at its first row and holds whole sequences of 2048 to 8192 rows one after another, each counted 0, 1, 2, ..., followed by its empty rows (-1), if any; groups hold different numbers of rows; some sequence has exactly 8192 rows. `dt_bias`: each entry is log(exp(dt) - 1) for a step dt between 0.01 / 8192 and 0.1.
All inputs are finite; a program needn't handle non-finite values.
Results may differ from a plain program's by a relative error of at most 0.0078.
Values may be sent and summed in bfloat16 or wider, within the bound.
A program may use at most 256 MiB of HBM per device.

v0:
```python
import jax
import jax.numpy as jnp
from jax import lax
from jax.sharding import PartitionSpec as P

INNER = 1536
BLOCK = 256


EPS = 1e-05
HIGHEST = lax.Precision.HIGHEST


def passed_along(value, axis, steps):
    count = lax.axis_size(axis)
    initial, last = (max(0, -steps), min(count, count - steps))
    return lax.ppermute(value, axis, [(source, source + steps) for source in range(initial, last)])


def entering(value, axis, join, neutral, backward):
    count, mine = (lax.axis_size(axis), lax.axis_index(axis))
    pieces = jax.tree.map(lambda part: lax.all_gather(part, axis), value)
    if backward:
        pieces = jax.tree.map(lambda part: part[::-1], pieces)
        mine = count - 1 - mine
    subtotal = jax.tree.map(
        lambda part, zero: jnp.full_like(part, 0) + jnp.asarray(zero, part.dtype), value, neutral
    )

    def turn(position, subtotal):
        longer = join(subtotal, jax.tree.map(lambda part: part[position], pieces))
        return jax.tree.map(lambda new, old: jnp.where(position < mine, new, old), longer, subtotal)

    return lax.fori_loop(0, count - 1, turn, subtotal)


def silu_grad(values):
    logistic = jax.nn.sigmoid(values)
    return logistic * (1.0 + values * (1.0 - logistic))


def contract_last(left, right):
    return lax.dot_general(
        left, right, (((1,), (1,)), ((), ())), preferred_element_type=jnp.float32
    )


def contract_rows(left, right):
    return lax.dot_general(
        left, right, (((0,), (0,)), ((), ())), preferred_element_type=jnp.float32
    )


def causal_conv(extended, weight, biases, positions):
    row_count = positions.shape[0]
    tap_count = weight.shape[0]
    totals = jnp.broadcast_to(biases[None, :], (row_count, biases.shape[0]))
    for offset in range(tap_count):
        window = lax.slice_in_dim(
            extended, tap_count - 1 - offset, tap_count - 1 - offset + row_count, axis=0
        )
        masked = (positions >= offset).astype(jnp.float32)[:, None]
        totals = totals + weight[offset][None, :] * window * masked
    return totals


def conv_back(grads_pre, extended, weight, positions):
    row_count = positions.shape[0]
    tap_count = weight.shape[0]
    spread = jnp.zeros((row_count + tap_count - 1, grads_pre.shape[1]), jnp.float32)
    weight_grads = []
    for offset in range(tap_count):
        masked = grads_pre * (positions >= offset).astype(jnp.float32)[:, None]
        window = lax.slice_in_dim(
            extended, tap_count - 1 - offset, tap_count - 1 - offset + row_count, axis=0
        )
        weight_grads.append(jnp.sum(masked * window, axis=0))
        spread = spread.at[tap_count - 1 - offset : tap_count - 1 - offset + row_count].add(
            weight[offset][None, :] * masked
        )
    return (jnp.stack(weight_grads), jnp.sum(grads_pre, axis=0), spread)


def block_weights(decay_log, state_b, state_c, starts):
    block_rows = starts.shape[0]
    cumulative = jnp.cumsum(decay_log, axis=1)
    segment = jnp.cumsum(starts)
    row_index = jnp.arange(block_rows)
    same_seq = jnp.logical_and(
        row_index[:, None] >= row_index[None, :], segment[:, None] == segment[None, :]
    )[None]
    spread = cumulative[:, :, None] - cumulative[:, None, :]
    within = jnp.where(same_seq, jnp.exp(jnp.where(same_seq, spread, 0.0)), 0.0)
    scores = lax.dot_general(state_c, state_b, (((1,), (1,)), ((), ())), precision=HIGHEST)
    entry_decay = jnp.exp(cumulative) * (segment == 0).astype(jnp.float32)[None, :]
    closing = (segment == segment[-1])[None, :]
    towards = jnp.where(closing, jnp.exp(cumulative[:, -1:] - cumulative), 0.0)
    through = jnp.exp(cumulative[:, -1]) * (segment[-1] == 0).astype(jnp.float32)
    return (within, scores, entry_decay, towards, through)


def block_local(decay_log, inner_u, state_b, state_c, starts):
    within, scores, entry_decay, towards, through = block_weights(
        decay_log, state_b, state_c, starts
    )
    intra_out = jnp.einsum("hij,jhp->ihp", within * scores[None], inner_u, precision=HIGHEST)
    local_state = jnp.einsum("hj,jhp,jn->hpn", towards, inner_u, state_b, precision=HIGHEST)
    return (intra_out, entry_decay, through, local_state)


def block_back(decay_log, inner_u, state_b, state_c, starts, grad_y, block_in, grad_out):
    within, scores, entry_decay, towards, through = block_weights(
        decay_log, state_b, state_c, starts
    )
    mixing = within * scores[None]
    grad_u = jnp.einsum("hij,ihp->jhp", mixing, grad_y, precision=HIGHEST)
    grad_u = grad_u + jnp.einsum("hj,hpn,jn->jhp", towards, grad_out, state_b, precision=HIGHEST)
    grad_mix = jnp.einsum("ihp,jhp->hij", grad_y, inner_u, precision=HIGHEST)
    grad_scores = jnp.sum(grad_mix * within, axis=0)
    pulled = grad_mix * scores[None] * within
    grad_cum = jnp.sum(pulled, axis=2) - jnp.sum(pulled, axis=1)
    grad_c = jnp.dot(grad_scores, state_b, precision=HIGHEST) + jnp.einsum(
        "hi,ihp,hpn->in", entry_decay, grad_y, block_in, precision=HIGHEST
    )
    grad_b = lax.dot_general(
        grad_scores, state_c, (((0,), (0,)), ((), ())), precision=HIGHEST
    ) + jnp.einsum("hj,hpn,jhp->jn", towards, grad_out, inner_u, precision=HIGHEST)
    grad_entry = jnp.einsum("ihp,hpn,in->hi", grad_y, block_in, state_c, precision=HIGHEST)
    grad_cum = grad_cum + grad_entry * entry_decay
    grad_towards = jnp.einsum("hpn,jhp,jn->hj", grad_out, inner_u, state_b, precision=HIGHEST)
    moved_back = grad_towards * towards
    grad_cum = grad_cum - moved_back
    closing_total = (
        jnp.sum(moved_back, axis=1) + jnp.sum(grad_out * block_in, axis=(1, 2)) * through
    )
    grad_cum = grad_cum.at[:, -1].add(closing_total)
    grad_decay = jnp.flip(jnp.cumsum(jnp.flip(grad_cum, axis=1), axis=1), axis=1)
    return (grad_u, grad_decay, grad_b, grad_c)


def local_item(block_item):
    return block_local(*block_item)


def back_item(block_item):
    return block_back(*block_item)


def chain_link(carry, block_item):
    factor, running = carry
    link_decay, link_state = block_item
    return (
        (factor * link_decay, link_decay[:, None, None] * running + link_state),
        (factor, running),
    )


def join_states(earlier, later):
    return (earlier[0] * later[0], later[0][:, None, None] * earlier[1] + later[1])


def on_device(
    hidden_in,
    cotangent,
    positions,
    norm_gain,
    proj_z,
    proj_x,
    proj_bc,
    proj_dt,
    conv_inner,
    conv_inner_bias,
    conv_state,
    conv_state_bias,
    dt_bias,
    a_log,
    skip_gain,
    gated_gain,
    proj_out,
):
    row_count = hidden_in.shape[0]
    full_width = hidden_in.shape[1]
    tap_count = conv_inner.shape[0]
    rim_rows = tap_count - 1
    local_inner = proj_z.shape[1]
    local_heads = proj_dt.shape[1]
    head_width = local_inner // local_heads
    state_width = proj_bc.shape[1] // 2
    block_count = row_count // BLOCK
    gathered = (
        lax.all_gather(norm_gain, ("fsdp", "ctx"), axis=0, tiled=True),
        lax.all_gather(proj_z, ("fsdp", "ctx"), axis=0, tiled=True),
        lax.all_gather(proj_x, ("fsdp", "ctx"), axis=0, tiled=True),
        lax.all_gather(proj_bc, ("fsdp", "ctx"), axis=0, tiled=True),
        lax.all_gather(proj_dt, ("fsdp", "ctx"), axis=0, tiled=True),
        lax.all_gather(proj_out, ("fsdp", "ctx"), axis=1, tiled=True),
    )
    gain_full, weight_z, weight_x, weight_bc, weight_dt, weight_out = gathered
    row_valid = (positions >= 0).astype(jnp.float32)
    starts = (positions == 0).astype(jnp.float32)
    hidden = hidden_in.astype(jnp.float32)
    row_scale = lax.rsqrt(jnp.mean(hidden * hidden, axis=1, keepdims=True) + EPS)
    normed = (hidden * row_scale * gain_full.astype(jnp.float32)[None, :]).astype(jnp.bfloat16)
    gate_z = jnp.dot(normed, weight_z, preferred_element_type=jnp.float32)
    inner_x = jnp.dot(normed, weight_x, preferred_element_type=jnp.float32)
    state_in = jnp.dot(normed, weight_bc, preferred_element_type=jnp.float32)
    step_raw = jnp.dot(normed, weight_dt, preferred_element_type=jnp.float32)
    rim_x, rim_bc = passed_along(
        (inner_x[row_count - rim_rows :], state_in[row_count - rim_rows :]), "ctx", 1
    )
    ext_x = jnp.concatenate([rim_x, inner_x], axis=0)
    ext_bc = jnp.concatenate([rim_bc, state_in], axis=0)
    pre_x = causal_conv(ext_x, conv_inner, conv_inner_bias, positions)
    pre_bc = causal_conv(ext_bc, conv_state, conv_state_bias, positions)
    conv_x = jax.nn.silu(pre_x)
    conv_bc = jax.nn.silu(pre_bc)
    state_b = conv_bc[:, :state_width]
    state_c = conv_bc[:, state_width:]
    shifted_step = step_raw + dt_bias[None, :]
    step_size = jax.nn.softplus(shifted_step)
    decay_rate = -jnp.exp(a_log)
    decay_log = step_size * decay_rate[None, :]
    heads_x = conv_x.reshape(row_count, local_heads, head_width)
    inner_u = heads_x * step_size[:, :, None]
    decay_blocks = decay_log.reshape(block_count, BLOCK, local_heads).transpose(0, 2, 1)
    u_blocks = inner_u.reshape(block_count, BLOCK, local_heads, head_width)
    b_blocks = state_b.reshape(block_count, BLOCK, state_width)
    c_blocks = state_c.reshape(block_count, BLOCK, state_width)
    start_blocks = starts.reshape(block_count, BLOCK)
    intra_out, entry_decay, through, local_state = lax.map(
        local_item, (decay_blocks, u_blocks, b_blocks, c_blocks, start_blocks)
    )
    ones_init = jnp.ones((local_heads,), jnp.float32)
    zeros_init = jnp.zeros((local_heads, head_width, state_width), jnp.float32)
    (piece_decay, piece_state), (prefix_decay, prefix_state) = lax.scan(
        chain_link, (ones_init, zeros_init), (through, local_state)
    )
    incoming_decay, incoming_state = entering(
        (piece_decay, piece_state), "ctx", join_states, (ones_init, zeros_init), False
    )
    block_in = prefix_decay[:, :, None, None] * incoming_state[None] + prefix_state
    carried = (
        jnp.einsum("chpn,cin->cihp", block_in, c_blocks, precision=HIGHEST)
        * jnp.transpose(entry_decay, (0, 2, 1))[:, :, :, None]
    )
    scanned = (intra_out + carried).reshape(row_count, local_heads, head_width)
    mixed_out = (scanned + skip_gain[None, :, None] * heads_x).reshape(row_count, local_inner)
    gate_act = jax.nn.silu(gate_z)
    gated_out = mixed_out * gate_act
    squares = lax.psum(jnp.sum(gated_out * gated_out, axis=1), "tp")
    gated_scale = lax.rsqrt(squares / INNER + EPS)[:, None]
    gnormed = (gated_out * gated_scale * gated_gain[None, :]).astype(jnp.bfloat16)
    partial_branch = jnp.dot(gnormed, weight_out, preferred_element_type=jnp.float32)
    branch = lax.psum(partial_branch, "tp")
    hidden_out = (hidden + branch * row_valid[:, None]).astype(jnp.bfloat16)
    weights_back = (
        lax.all_gather(norm_gain, ("fsdp", "ctx"), axis=0, tiled=True),
        lax.all_gather(proj_z, ("fsdp", "ctx"), axis=0, tiled=True),
        lax.all_gather(proj_x, ("fsdp", "ctx"), axis=0, tiled=True),
        lax.all_gather(proj_bc, ("fsdp", "ctx"), axis=0, tiled=True),
        lax.all_gather(proj_dt, ("fsdp", "ctx"), axis=0, tiled=True),
        lax.all_gather(proj_out, ("fsdp", "ctx"), axis=1, tiled=True),
    )
    gain_back, again_z, again_x, again_bc, again_dt, again_out = weights_back
    grad_branch = (cotangent.astype(jnp.float32) * row_valid[:, None]).astype(jnp.bfloat16)
    grad_wout = contract_rows(gnormed, grad_branch)
    grad_gnormed = contract_last(grad_branch, again_out)
    weighted = grad_gnormed * gated_gain[None, :]
    grad_ggain = jnp.sum(grad_gnormed * gated_out * gated_scale, axis=0)
    gated_dot = lax.psum(jnp.sum(weighted * gated_out, axis=1), "tp")[:, None]
    grad_gated = gated_scale * weighted - gated_out * gated_scale**3 * gated_dot / INNER
    grad_mixed = grad_gated * gate_act
    grad_z = (grad_gated * mixed_out * silu_grad(gate_z)).astype(jnp.bfloat16)
    grad_y = grad_mixed.reshape(row_count, local_heads, head_width)
    grad_skip = jnp.sum(grad_y * heads_x, axis=(0, 2))
    grad_y_blocks = grad_y.reshape(block_count, BLOCK, local_heads, head_width)
    local_back = jnp.einsum(
        "chi,cihp,cin->chpn", entry_decay, grad_y_blocks, c_blocks, precision=HIGHEST
    )
    (piece_factor, piece_back), (suffix_decay, suffix_back) = lax.scan(
        chain_link, (ones_init, zeros_init), (through, local_back), reverse=True
    )
    outgoing_decay, outgoing_grad = entering(
        (piece_decay, piece_back), "ctx", join_states, (ones_init, zeros_init), True
    )
    grad_out_blocks = suffix_decay[:, :, None, None] * outgoing_grad[None] + suffix_back
    grad_u, grad_decay, grad_b, grad_c = lax.map(
        back_item,
        (
            decay_blocks,
            u_blocks,
            b_blocks,
            c_blocks,
            start_blocks,
            grad_y_blocks,
            block_in,
            grad_out_blocks,
        ),
    )
    grad_u = grad_u.reshape(row_count, local_heads, head_width)
    grad_decay = grad_decay.transpose(0, 2, 1).reshape(row_count, local_heads)
    grad_step = grad_decay * decay_rate[None, :] + jnp.sum(grad_u * heads_x, axis=2)
    grad_alog = jnp.sum(grad_decay * step_size, axis=0) * decay_rate
    grad_shift = grad_step * jax.nn.sigmoid(shifted_step)
    grad_dtbias = jnp.sum(grad_shift, axis=0)
    grad_raw = grad_shift.astype(jnp.bfloat16)
    grad_heads = grad_u * step_size[:, :, None] + skip_gain[None, :, None] * grad_y
    grad_pre_x = grad_heads.reshape(row_count, local_inner) * silu_grad(pre_x)
    grad_bc_part = jnp.concatenate(
        [grad_b.reshape(row_count, state_width), grad_c.reshape(row_count, state_width)], axis=1
    )
    grad_conv_bc = lax.psum(grad_bc_part, "tp")
    grad_pre_bc = grad_conv_bc * silu_grad(pre_bc)
    wgrad_x, bgrad_x, spread_x = conv_back(grad_pre_x, ext_x, conv_inner, positions)
    wgrad_bc, bgrad_bc, spread_bc = conv_back(grad_pre_bc, ext_bc, conv_state, positions)
    later_x, later_bc = passed_along((spread_x[:rim_rows], spread_bc[:rim_rows]), "ctx", -1)
    grad_inner_x = spread_x[rim_rows:].at[row_count - rim_rows :].add(later_x).astype(jnp.bfloat16)
    grad_state_in = (
        spread_bc[rim_rows:].at[row_count - rim_rows :].add(later_bc).astype(jnp.bfloat16)
    )
    first_tp = (lax.axis_index("tp") == 0).astype(jnp.float32)
    partial_grad = (
        contract_last(grad_z, again_z)
        + contract_last(grad_inner_x, again_x)
        + contract_last(grad_raw, again_dt)
        + first_tp * contract_last(grad_state_in, again_bc)
    )
    grad_normed = lax.psum(partial_grad, "tp")
    pulled = grad_normed * gain_back.astype(jnp.float32)[None, :]
    norm_dot = jnp.sum(pulled * hidden, axis=1, keepdims=True)
    grad_hidden = (
        row_scale * pulled
        - hidden * row_scale**3 * norm_dot / full_width
        + cotangent.astype(jnp.float32)
    )
    grad_gain = jnp.sum(grad_normed * hidden * row_scale, axis=0)
    grad_wz = contract_rows(normed, grad_z)
    grad_wx = contract_rows(normed, grad_inner_x)
    grad_wbc = contract_rows(normed, grad_state_in)
    grad_wdt = contract_rows(normed, grad_raw)
    scattered = (
        lax.psum_scatter(grad_gain, ("fsdp", "ctx"), scatter_dimension=0, tiled=True),
        lax.psum_scatter(grad_wz, ("fsdp", "ctx"), scatter_dimension=0, tiled=True),
        lax.psum_scatter(grad_wx, ("fsdp", "ctx"), scatter_dimension=0, tiled=True),
        lax.psum_scatter(grad_wbc, ("fsdp", "ctx"), scatter_dimension=0, tiled=True),
        lax.psum_scatter(grad_wdt, ("fsdp", "ctx"), scatter_dimension=0, tiled=True),
        lax.psum_scatter(grad_wout, ("fsdp", "ctx"), scatter_dimension=1, tiled=True),
    )
    reduced_small = lax.psum(
        (grad_ggain, wgrad_x, bgrad_x, wgrad_bc, bgrad_bc, grad_dtbias, grad_alog, grad_skip),
        ("fsdp", "ctx"),
    )
    return (
        hidden_out,
        grad_hidden,
        scattered[0],
        scattered[1],
        scattered[2],
        scattered[3],
        scattered[4],
        reduced_small[1],
        reduced_small[2],
        reduced_small[3],
        reduced_small[4],
        reduced_small[5],
        reduced_small[6],
        reduced_small[7],
        reduced_small[0],
        scattered[5],
    )


def solution(mesh):
    placed = (
        P(("fsdp", "ctx"), None),
        P(("fsdp", "ctx"), None),
        P(("fsdp", "ctx")),
        P(("fsdp", "ctx")),
        P(("fsdp", "ctx"), "tp"),
        P(("fsdp", "ctx"), "tp"),
        P(("fsdp", "ctx"), None),
        P(("fsdp", "ctx"), "tp"),
        P(None, "tp"),
        P("tp"),
        P(),
        P(),
        P("tp"),
        P("tp"),
        P("tp"),
        P("tp"),
        P("tp", ("fsdp", "ctx")),
    )
    return jax.shard_map(
        on_device,
        mesh=mesh,
        in_specs=placed,
        out_specs=(
            P(("fsdp", "ctx"), None),
            P(("fsdp", "ctx"), None),
            P(("fsdp", "ctx")),
            P(("fsdp", "ctx"), "tp"),
            P(("fsdp", "ctx"), "tp"),
            P(("fsdp", "ctx"), None),
            P(("fsdp", "ctx"), "tp"),
            P(None, "tp"),
            P("tp"),
            P(),
            P(),
            P("tp"),
            P("tp"),
            P("tp"),
            P("tp"),
            P("tp", ("fsdp", "ctx")),
        ),
        check_vma=False,
    )
```

profile of v0, /device:TPU:0, one launch (start us, length us, event | category | flops | bytes accessed | tf_op | source)
XLA Modules:
  0.0 1959.8 jit_solution(11732612440422561694)
XLA Ops:
  10.8 43.5 %all-reduce.2 = bf16[768]{0:T(1024)(128)(2,1)S(1)} all-reduce(bf16[768]{0:T(1024)(128)(2,1)S(1)} %dynamic-update-slice.36), channel_id=1, replica_groups=mesh['fsdp'=4,'ctx'=4,'tp'=2] {'fsdp','ctx'}, use_global_device_ids=true, to_apply=%add.2 | all-reduce | flops 768 | bytes 3072
  57.7 38.4 %all_gather.47 = bf16[768,256]{1,0:T(8,128)(2,1)S(1)} all-gather(bf16[48,256]{1,0:T(8,128)(2,1)} %param.57), channel_id=1, replica_groups=mesh['fsdp'=4,'ctx'=4,'tp'=2] {'fsdp','ctx'}, dimensions={0}, use_global_device_ids=true | all-gather | bytes 417792 | tf_op jit(solution)/shard_map/all_gather | solution.py:194
  106.3 35.8 %all-gather.3 = bf16[16,48,12]{1,2,0:T(8,128)(2,1)S(1)} all-gather(bf16[1,48,12]{1,2,0:T(8,128)(2,1)S(1)} %bitcast.459), channel_id=1, replica_groups=mesh['fsdp'=4,'ctx'=4,'tp'=2] {'fsdp','ctx'}, dimensions={0}, use_global_device_ids=true | all-gather | bytes 19584 | tf_op jit(solution)/shard_map/all_gather | solution.py:195
  201.1 221.2 %while.112 = (s32[]{:T(128)}, f32[8,256,12,64]{1,3,2,0:T(8,128)}, f32[8,12,256]{2,1,0:T(8,128)}, f32[8,12]{1,0:T(8,128)}, f32[8,12,64,128]{3,2,1,0:T(8,128)}, /*...) while((s32[]{:T(128)}, f32[8,256,12,64]{1,3,2,0:T(8,128)}, ...), condition=%wide.region_6.7_spmd, body=%wide.region_1.6_spmd.sunk | while | flops 1010607872 | bytes 4239135 | solution.py:230
  424.3 25.3 %while.114 = (s32[]{:T(128)}, f32[12]{0:T(128)}, f32[12,64,128]{2,1,0:T(8,128)S(1)}, f32[8,12]{1,0:T(8,128)S(1)}, f32[8,12,64,128]{3,2,1,0:T(8,128)}, /*index=5*...) while((s32[]{:T(128)}, f32[12]{0:T(128)}, f32[12,64,128]{2,1,0:T(8,128)S(1)}, ...), condition=%wide.region_8.9_spmd.clone, body=%wide.region_7.8_spmd.clone.sunk | while | flops 393243 | bytes 1967093 | solution.py:235
  454.1 9.4 all-reduce.3
  463.6 15.5 all-gather.16.cloned.1.call-done
  514.1 23.9 %all-gather.12.cloned.1.call-done = bf16[768,768]{1,0:T(8,128)(2,1)} async-done(((bf16[48,768]{1,0:T(8,128)(2,1)}), bf16[768,768]{1,0:T(8,128)(2,1)}) %all-gather.12.cloned.1.call-update) | async-done | bytes 1179664 | tf_op jit(solution)/shard_map/all_gather | solution.py:192
  538.1 11.1 multiply_reduce_fusion.10
  551.8 44.0 %all-gather.14.cloned.1.call-done = bf16[768,768]{0,1:T(8,128)(2,1)} async-done(((bf16[768,48]{0,1:T(8,128)(2,1)}), bf16[768,768]{0,1:T(8,128)(2,1)}) %all-gather.14.cloned.1.call-update) | async-done | bytes 1179664 | tf_op jit(solution)/shard_map/all_gather | solution.py:196
  606.6 17.1 multiply_reduce_fusion.3
  647.1 21.1 %while.116 = (s32[]{:T(128)}, f32[12]{0:T(128)S(1)}, f32[12,64,128]{2,1,0:T(8,128)S(1)}, f32[8,12]{1,0:T(8,128)S(1)}, f32[8,12,64,128]{3,2,1,0:T(8,128)}, /*inde...) while((s32[]{:T(128)}, f32[12]{0:T(128)S(1)}, ...), condition=%wide.region_17.18_spmd.clone, body=%wide.region_16.17_spmd.clone.sunk | while | flops 393244 | bytes 1966605 | solution.py:280
  705.6 436.0 %while.113 = (s32[]{:T(128)}, f32[8,256,12,64]{1,0,3,2:T(8,128)}, f32[8,12,256]{2,1,0:T(8,128)}, f32[8,256,128]{2,1,0:T(8,128)S(1)}, f32[8,256,128]{2,1,0:T(8,12...) while((s32[]{:T(128)}, f32[8,256,12,64]{1,0,3,2:T(8,128)}, ...), condition=%wide.region_33.34_spmd, body=%wide.region_21.33_spmd.sunk | while | flops 2730934016 | bytes 17460180 | solution.py:287
  733.9 18.5 dynamic_update_slice.96
  788.3 18.5 dynamic_update_slice.96
  842.8 18.5 dynamic_update_slice.96
  897.3 18.5 dynamic_update_slice.96
  951.7 18.5 dynamic_update_slice.96
  1006.2 18.5 dynamic_update_slice.96
  1060.6 18.5 dynamic_update_slice.96
  1115.1 18.5 dynamic_update_slice.96
  1159.8 20.9 %multiply_reduce_fusion.6 = (f32[768]{0:T(1024)S(1)}, f32[768]{0:T(1024)S(1)}, f32[768]{0:T(1024)S(1)}, f32[768]{0:T(1024)S(1)}, f32[768]{0:T(1024)S(1)}, /*index=5*/f32[2048,768]{1,0:T(8,128)S(1)}) fusion(f32[2048]{0:T(1024)S(1)} %copy-done.38, f32[2048,768]{1,0:T(8,128)} %copy-done.12, f32[3,768]{1,0:T(4,128)S(1)} %copy-done.47, f32[2048]{0:T(1024)S(1)} %copy-done.36, ...), kind=kLoop, calls=%fused_computation.192 | loop fusion | flops 42463488 | bytes 37809152 | tf_op jit(solution)/shard_map/reduce_sum | solution.py:77
  1189.6 16.1 scatter-add.40
  1213.1 16.2 scatter-add.41
  1291.8 10.7 multiply_add_fusion
  1329.1 46.6 %reduce-scatter.16.cloned.1.call-done = f32[48,12]{1,0:T(8,128)} async-done(((f32[768,12]{1,0:T(8,128)}), f32[48,12]{1,0:T(8,128)}) %reduce-scatter.16.cloned.1.call-update) | async-done | bytes 2320
  1377.2 49.7 %all-reduce.12.cloned.1.call-done = (f32[2048,768]{1,0:T(8,128)}, f32[2048,768]{1,0:T(8,128)}) async-done(((f32[2048,768]{1,0:T(8,128)}, f32[2048,768]{1,0:T(8,128)}), (f32[2048,768]{1,0:T(8,128)}, f32[2048,768]{1,0:T(8,128)})) %all-reduce.12.cloned.1.call-update) | async-done | bytes 12582928 | tf_op jit(solution)/shard_map/psum | solution.py:254
  1431.1 77.9 %all-reduce.5 = (f32[768]{0:T(1024)S(1)}, f32[4,768]{1,0:T(4,128)}, f32[768]{0:T(1024)}, f32[4,256]{1,0:T(4,128)}, f32[256]{0:T(256)}, /*index=5*/f32[12]{0:T(128)}, f32[12]{0:T(128)}, f32[12]{0:T(128)}, f32[768]{0:T(1024)}) all-reduce(f32[768]{0:T(1024)S(1)} %get-tuple-element.1008, ...), channel_id=5, replica_groups=mesh['fsdp'=4,'ctx'=4,'tp'=2] {'fsdp','ctx'}, use_global_device_ids=true, to_apply=%region_39.40.clone | all-reduce | flops 6692 | bytes 53536
  1518.8 42.5 %reduce-scatter.14.cloned.1.call-done = f32[768,48]{0,1:T(8,128)} async-done(((f32[768,768]{0,1:T(8,128)}), f32[768,48]{0,1:T(8,128)}) %reduce-scatter.14.cloned.1.call-update) | async-done | bytes 147472 | tf_op jit(solution)/shard_map/reduce_scatter | solution.py:347
  1561.3 132.8 %reduce-scatter.8.cloned.1.call-done = f32[48,768]{1,0:T(8,128)} async-done(((f32[768,768]{1,0:T(8,128)}), f32[48,768]{1,0:T(8,128)}) %reduce-scatter.8.cloned.1.call-update) | async-done | bytes 147472 | tf_op jit(solution)/shard_map/reduce_scatter | solution.py:343
  1694.1 126.6 %reduce-scatter.12.cloned.1.call-done = f32[48,256]{1,0:T(8,128)} async-done(((f32[768,256]{1,0:T(8,128)}), f32[48,256]{1,0:T(8,128)}) %reduce-scatter.12.cloned.1.call-update) | async-done | bytes 49168 | tf_op jit(solution)/shard_map/reduce_scatter | solution.py:345
  1820.7 132.1 %reduce-scatter.10.cloned.1.call-done = f32[48,768]{1,0:T(8,128)} async-done(((f32[768,768]{1,0:T(8,128)}), f32[48,768]{1,0:T(8,128)}) %reduce-scatter.10.cloned.1.call-update) | async-done | bytes 147472 | tf_op jit(solution)/shard_map/reduce_scatter | solution.py:344
  (1084 shorter events, 876.8 us)
Async XLA Ops:
  7.2 152.3 %all-gather.10.cloned.1.call-start = ((), (), s32[]{:S(2)}) async-start(), calls=%async_computation.5 | async-start | bytes 1253376 | tf_op jit(solution)/shard_map/all_gather | solution.py:193
  7.9 471.2 %all-gather.16.cloned.1.call-start = ((), (), s32[]{:S(2)}) async-start(), calls=%async_computation.13 | async-start | bytes 1966080 | tf_op jit(solution)/shard_map/all_gather | solution.py:22
  54.3 45.7 %copy-start.44 = (f32[768]{0:T(1024)}, f32[768]{0:T(1024)S(1)}, u32[]{:S(2)}) copy-start(f32[768]{0:T(1024)S(1)} %convert_element_type.91) | copy-start | bytes 9220
  96.0 46.2 %copy-start.84 = (f32[12]{0:T(128)S(1)}, f32[12]{0:T(128)}, u32[]{:S(2)}) copy-start(f32[12]{0:T(128)} %param.64) | copy-start | bytes 148
  96.1 46.2 %copy-start.79 = (f32[12]{0:T(128)S(1)}, f32[12]{0:T(128)}, u32[]{:S(2)}) copy-start(f32[12]{0:T(128)} %param.63) | copy-start | bytes 148
  98.9 439.1 %copy-start.4 = (bf16[2048,768]{1,0:T(8,128)(2,1)}, bf16[2048,768]{1,0:T(8,128)(2,1)S(1)}, u32[]{:S(2)}) copy-start(bf16[2048,768]{1,0:T(8,128)(2,1)S(1)} %fusion.121) | copy-start | bytes 9437188
  98.9 45.8 %copy-start.78 = (f32[4,256]{1,0:T(4,128)S(1)}, f32[4,256]{1,0:T(4,128)}, u32[]{:S(2)}) copy-start(f32[4,256]{1,0:T(4,128)} %param.61) | copy-start | bytes 12292
  98.9 46.3 %copy-start.70 = (s32[2048]{0:T(1024)S(1)}, s32[2048]{0:T(1024)}, u32[]{:S(2)}) copy-start(s32[2048]{0:T(1024)} %param.53) | copy-start | bytes 24580
  98.9 48.2 %copy-start.63 = (f32[4,768]{1,0:T(4,128)S(1)}, f32[4,768]{1,0:T(4,128)}, u32[]{:S(2)}) copy-start(f32[4,768]{1,0:T(4,128)} %param.59) | copy-start | bytes 36868
  102.0 48.7 %collective-permute-start.1 = (f32[3,256]{1,0:T(4,128)}, f32[3,256]{1,0:T(4,128)}, u32[]{:S(2)}, u32[]{:S(2)}) collective-permute-start(f32[3,256]{1,0:T(4,128)} %slice.400), channel_id=1, source_target_pairs={{0,2},{2,4},{4,6},{1,3},{3,5},{5,7},{8,10},{10,12},{12,14},{9,11},... | collective-permute-start | bytes 9224 | tf_op jit(solution)/shard_map/ppermute | solution.py:17
  163.7 5.9 collective-permute-start
  450.4 87.6 %all-gather.12.cloned.1.call-start = ((), (), s32[]{:S(2)}) async-start(), calls=%async_computation.6 | async-start | bytes 1253376 | tf_op jit(solution)/shard_map/all_gather | solution.py:192
  451.2 144.6 %all-gather.14.cloned.1.call-start = ((), (), s32[]{:S(2)}) async-start(), calls=%async_computation.7 | async-start | bytes 1253376 | tf_op jit(solution)/shard_map/all_gather | solution.py:196
  451.8 247.2 %all-gather.18.cloned.1.call-start = ((), (), s32[]{:S(2)}) async-start(), calls=%async_computation.14 | async-start | bytes 1966080 | tf_op jit(solution)/shard_map/all_gather | solution.py:22
  452.6 154.0 %copy-start.56 = (f32[768]{0:T(1024)}, f32[768]{0:T(1024)S(1)}, u32[]{:S(2)}) copy-start(f32[768]{0:T(1024)S(1)} %mul.828) | copy-start | bytes 9220
  538.0 57.7 %copy-start.29 = (f32[2048]{0:T(1024)S(1)}, f32[2048]{0:T(1024)}, u32[]{:S(2)}) copy-start(f32[2048]{0:T(1024)} %copy-done.28) | copy-start | bytes 24580
  538.0 57.7 %copy-start.74 = (f32[768]{0:T(1024)S(1)}, f32[768]{0:T(1024)}, u32[]{:S(2)}) copy-start(f32[768]{0:T(1024)} %param.66) | copy-start | bytes 9220
  551.8 140.8 %copy-start.59 = (f32[2048]{0:T(1024)}, f32[2048]{0:T(1024)S(1)}, u32[]{:S(2)}) copy-start(f32[2048]{0:T(1024)S(1)} %get-tuple-element.1172) | copy-start | bytes 24580
  669.0 583.9 %all-reduce.10.cloned.1.call-start = ((), (), s32[]{:S(2)}) async-start(), calls=%async_computation.8 | async-start | bytes 4194304 | tf_op jit(solution)/shard_map/psum | solution.py:312
  1144.3 231.5 %reduce-scatter.16.cloned.1.call-start = ((), (), s32[]{:S(2)}) async-start(), calls=%async_computation.15 | async-start | bytes 417792
  1237.1 14.9 collective-permute-start.2
  1251.9 175.0 %all-reduce.12.cloned.1.call-start = ((), (), s32[]{:S(2)}) async-start(), calls=%async_computation.16 | async-start | bytes 25165824 | tf_op jit(solution)/shard_map/psum | solution.py:254
  1285.4 6.3 collective-permute-start.3
  1302.5 258.8 %reduce-scatter.14.cloned.1.call-start = ((), (), s32[]{:S(2)}) async-start(), calls=%async_computation.12 | async-start | bytes 2506752 | tf_op jit(solution)/shard_map/reduce_scatter | solution.py:347
  1311.7 382.5 %reduce-scatter.8.cloned.1.call-start = ((), (), s32[]{:S(2)}) async-start(), calls=%async_computation.9 | async-start | bytes 2506752 | tf_op jit(solution)/shard_map/reduce_scatter | solution.py:343
  1317.8 502.9 %reduce-scatter.12.cloned.1.call-start = ((), (), s32[]{:S(2)}) async-start(), calls=%async_computation.11 | async-start | bytes 835584 | tf_op jit(solution)/shard_map/reduce_scatter | solution.py:345
  1321.0 105.9 %copy-start.3 = (bf16[2048,768]{1,0:T(8,128)(2,1)S(1)}, bf16[2048,768]{1,0:T(8,128)(2,1)}, u32[]{:S(2)}) copy-start(bf16[2048,768]{1,0:T(8,128)(2,1)} %param.51) | copy-start | bytes 9437188
  1321.0 105.9 %copy-start.43 = (f32[2048]{0:T(1024)S(1)}, f32[2048]{0:T(1024)}, u32[]{:S(2)}) copy-start(f32[2048]{0:T(1024)} %copy-done.42) | copy-start | bytes 24580
  1321.0 105.9 %copy-start.45 = (f32[768]{0:T(1024)S(1)}, f32[768]{0:T(1024)}, u32[]{:S(2)}) copy-start(f32[768]{0:T(1024)} %copy-done.44) | copy-start | bytes 9220
  1321.0 631.8 %reduce-scatter.10.cloned.1.call-start = ((), (), s32[]{:S(2)}) async-start(), calls=%async_computation.10 | async-start | bytes 2506752 | tf_op jit(solution)/shard_map/reduce_scatter | solution.py:344
  1328.2 102.9 %copy-start.77 = (f32[768]{0:T(1024)S(1)}, f32[768]{0:T(1024)}, u32[]{:S(2)}) copy-start(f32[768]{0:T(1024)} %get-tuple-element.1005) | copy-start | bytes 9220
  1328.2 181.4 %copy-start.58 = (f32[2048]{0:T(1024)S(1)}, f32[2048]{0:T(1024)}, u32[]{:S(2)}) copy-start(f32[2048]{0:T(1024)} %get-tuple-element.1169) | copy-start | bytes 24580
  (89 other events, 787.8 us)
Sparse Core Ops, SparseCore 0:
  10.8 59.3 all-gather.9
  450.6 28.4 all-gather.15
  481.9 56.1 all-gather.11
  540.7 55.0 all-gather.13
  669.1 29.8 all-gather.17
  1144.4 21.2 all-reduce.9
  1252.0 123.6 reduce-scatter.15
  1378.3 48.5 all-reduce.11
  1432.4 128.8 reduce-scatter.13
  1567.4 126.6 reduce-scatter.7
  1699.4 121.2 reduce-scatter.11
  1826.1 126.6 reduce-scatter.9
where the time goes:
time: 1980 us; the launch traced here: 1960 us
  waiting for transfers between devices  618 us (31%)
  local copies, waits for them, and re-layouts  435 us (22%)
  matrix products  360 us (18%)
  other arithmetic  294 us (15%)
  blocking collectives  210 us (11%)
    dynamic_update_slice x48, local copies, waits for them, and re-layouts, on_device(): lax.map(local_item, (decay_blocks, u_blocks, b_blocks, c_blocks, start_bl...  170 us
    reduce_scatter x1, waiting for transfers between devices, on_device(): lax.psum_scatter(grad_wz, ('fsdp', 'ctx'), scatter_dimension=0, tiled=True)  133 us
    reduce_scatter x1, waiting for transfers between devices, on_device(): lax.psum_scatter(grad_wx, ('fsdp', 'ctx'), scatter_dimension=0, tiled=True)  132 us
    unnamed x3, blocking collectives  131 us
    reduce_scatter x1, waiting for transfers between devices, on_device(): lax.psum_scatter(grad_wbc, ('fsdp', 'ctx'), scatter_dimension=0, tiled=True)  127 us
    scatter-add x6, local copies, waits for them, and re-layouts, conv_back(): spread.at[tap_count - 1 - offset:tap_count - 1 - offset + row_count]  49.8 us
    psum x1, waiting for transfers between devices, on_device(): branch = lax.psum(partial_branch, 'tp')  49.7 us
    another operation x109, other arithmetic  49 us
  transfers between devices with their start and end apart: 16, of which 10 were waited for; matrix products, arithmetic and copies ran while one was open for 15% of the time, Pallas kernels for 0%

commit v1 on v0

v1 whole, which is shorter than its diff:
```python
import functools

import jax
import jax.numpy as jnp
from jax import lax
from jax.experimental import pallas as pl
from jax.experimental.pallas import tpu as pltpu
from jax.sharding import PartitionSpec as P

INNER = 1536
BLOCK = 256


EPS = 1e-05
HIGHEST = lax.Precision.HIGHEST


def passed_along(value, axis, steps):
    count = lax.axis_size(axis)
    initial, last = (max(0, -steps), min(count, count - steps))
    return lax.ppermute(value, axis, [(source, source + steps) for source in range(initial, last)])


def pair_sum(value, axis):
    if lax.axis_size(axis) != 2:
        return lax.psum(value, axis)
    return value + lax.ppermute(value, axis, [(0, 1), (1, 0)])


def entering(decay, state, axis, backward):
    count, mine = (lax.axis_size(axis), lax.axis_index(axis))
    decays, states = (lax.all_gather(decay, axis), lax.all_gather(state, axis))
    running = jnp.zeros_like(state)
    for step in range(count - 1):
        at = count - 1 - step if backward else step
        joined = decays[at] * running + states[at]
        running = jnp.where(at > mine if backward else at < mine, joined, running)
    return running


def silu_grad(values):
    logistic = jax.nn.sigmoid(values)
    return logistic * (1.0 + values * (1.0 - logistic))


def contract_last(left, right):
    return lax.dot_general(
        left, right, (((1,), (1,)), ((), ())), preferred_element_type=jnp.float32
    )


def contract_rows(left, right):
    return lax.dot_general(
        left, right, (((0,), (0,)), ((), ())), preferred_element_type=jnp.float32
    )


def causal_conv(extended, weight, biases, positions):
    row_count = positions.shape[0]
    tap_count = weight.shape[0]
    totals = jnp.broadcast_to(biases[None, :], (row_count, biases.shape[0]))
    for offset in range(tap_count):
        window = lax.slice_in_dim(
            extended, tap_count - 1 - offset, tap_count - 1 - offset + row_count, axis=0
        )
        masked = (positions >= offset).astype(jnp.float32)[:, None]
        totals = totals + weight[offset][None, :] * window * masked
    return totals


def conv_back(grads_pre, extended, weight, positions):
    row_count = positions.shape[0]
    tap_count = weight.shape[0]
    spread = None
    weight_grads = []
    for offset in range(tap_count):
        masked = grads_pre * (positions >= offset).astype(jnp.float32)[:, None]
        window = lax.slice_in_dim(
            extended, tap_count - 1 - offset, tap_count - 1 - offset + row_count, axis=0
        )
        weight_grads.append(jnp.sum(masked * window, axis=0))
        term = jnp.pad(
            weight[offset][None, :] * masked, ((tap_count - 1 - offset, offset), (0, 0))
        )
        spread = term if spread is None else spread + term
    return (jnp.stack(weight_grads), jnp.sum(grads_pre, axis=0), spread)


NN = (((1,), (0,)), ((), ()))
NT = (((1,), (1,)), ((), ()))
TN = (((0,), (0,)), ((), ()))


def dot_full(left, right, dims):
    return lax.dot_general(
        left, right, dims, precision=HIGHEST, preferred_element_type=jnp.float32
    )


def first_half(rows, width):
    return lax.broadcasted_iota(jnp.int32, (rows, 2 * width), 1) < width


def spread_pair(factors, pair, first):
    return jnp.where(
        first, factors[:, 2 * pair : 2 * pair + 1], factors[:, 2 * pair + 1 : 2 * pair + 2]
    )


def state_kernel(width, factor_ref, left_ref, right_ref, out_ref):
    rows = left_ref.shape[0]
    first = first_half(rows, width)
    factors, right = (factor_ref[...], right_ref[...])
    for pair in range(factor_ref.shape[1] // 2):
        columns = slice(2 * width * pair, 2 * width * (pair + 1))
        scaled = left_ref[:, columns] * spread_pair(factors, pair, first)
        out_ref[columns, :] = dot_full(scaled, right, TN)


def allowed_bias(seg_col, seg_row):
    rows = seg_col.shape[0]
    later = lax.broadcasted_iota(jnp.int32, (rows, rows), 0)
    earlier = lax.broadcasted_iota(jnp.int32, (rows, rows), 1)
    allowed = jnp.logical_and(later >= earlier, seg_col == seg_row)
    return jnp.where(allowed, 0.0, -1e30)


def scan_kernel(
    width, cum_ref, cum_t_ref, seg_ref, seg_t_ref, entry_ref, u_ref, b_ref, c_ref, in_ref, out_ref
):
    rows = u_ref.shape[0]
    first = first_half(rows, width)
    state_c = c_ref[...]
    scores = dot_full(state_c, b_ref[...], NT)
    bias = allowed_bias(seg_ref[...], seg_t_ref[...])
    entry = entry_ref[...]
    for pair in range(entry_ref.shape[1] // 2):
        columns = slice(2 * width * pair, 2 * width * (pair + 1))
        inner_u = u_ref[:, columns]
        carried = dot_full(state_c, in_ref[columns, :], NT) * spread_pair(entry, pair, first)
        parts = []
        for head in (2 * pair, 2 * pair + 1):
            gap = cum_ref[:, head : head + 1] - cum_t_ref[head : head + 1, :]
            parts.append(dot_full(jnp.exp(gap + bias) * scores, inner_u, NN))
        out_ref[:, columns] = carried + jnp.where(first, parts[0], parts[1])


def back_kernel(
    width,
    cum_ref,
    cum_t_ref,
    seg_ref,
    seg_t_ref,
    entry_ref,
    towards_ref,
    u_ref,
    dy_ref,
    b_ref,
    c_ref,
    in_ref,
    out_grad_ref,
    grad_u_ref,
    grad_cum_ref,
    grad_cum_t_ref,
    grad_b_ref,
    grad_c_ref,
):
    rows = u_ref.shape[0]
    first = first_half(rows, width)
    state_b, state_c = (b_ref[...], c_ref[...])
    scores = dot_full(state_c, state_b, NT)
    bias = allowed_bias(seg_ref[...], seg_t_ref[...])
    entry, towards = (entry_ref[...], towards_ref[...])
    last_row = lax.broadcasted_iota(jnp.int32, (rows, 1), 0) == rows - 1
    grad_scores = jnp.zeros((rows, rows), jnp.float32)
    grad_b = jnp.zeros(state_b.shape, jnp.float32)
    grad_c = jnp.zeros(state_c.shape, jnp.float32)
    for pair in range(entry_ref.shape[1] // 2):
        columns = slice(2 * width * pair, 2 * width * (pair + 1))
        inner_u, grad_y = (u_ref[:, columns], dy_ref[:, columns])
        state_in, grad_out = (in_ref[columns, :], out_grad_ref[columns, :])
        entry_pair = spread_pair(entry, pair, first)
        towards_pair = spread_pair(towards, pair, first)
        from_later = dot_full(state_b, grad_out, NT)
        from_earlier = dot_full(state_c, state_in, NT)
        grad_c = grad_c + dot_full(entry_pair * grad_y, state_in, NN)
        grad_b = grad_b + dot_full(towards_pair * inner_u, grad_out, NN)
        later_dot = from_later * inner_u * towards_pair
        earlier_dot = from_earlier * grad_y * entry_pair
        parts = []
        for half in (0, 1):
            head = 2 * pair + half
            mine = first if half == 0 else jnp.logical_not(first)
            gap = cum_ref[:, head : head + 1] - cum_t_ref[head : head + 1, :]
            within = jnp.exp(gap + bias)
            parts.append(dot_full(within * scores, grad_y, TN))
            grad_mix = dot_full(jnp.where(mine, grad_y, 0.0), inner_u, NT) * within
            grad_scores = grad_scores + grad_mix
            pulled = grad_mix * scores
            moved = jnp.sum(jnp.where(mine, later_dot, 0.0), axis=1, keepdims=True)
            entered = jnp.sum(jnp.where(mine, earlier_dot, 0.0), axis=1, keepdims=True)
            total = jnp.sum(moved, axis=0, keepdims=True)
            grad_cum_ref[:, head : head + 1] = (
                jnp.sum(pulled, axis=1, keepdims=True)
                + entered
                - moved
                + jnp.where(last_row, total, 0.0)
            )
            grad_cum_t_ref[head : head + 1, :] = jnp.sum(pulled, axis=0, keepdims=True)
        grad_u_ref[:, columns] = (
            jnp.where(first, parts[0], parts[1]) + towards_pair * from_later
        )
    grad_b_ref[...] = grad_b + dot_full(grad_scores, state_c, TN)
    grad_c_ref[...] = grad_c + dot_full(grad_scores, state_b, NN)


def by_blocks(kernel, operands, outs, block_count):
    def spec(shape):
        return pl.BlockSpec((None, *shape[1:]), lambda at: (at,) + (0,) * (len(shape) - 1))

    return pl.pallas_call(
        kernel,
        grid=(block_count,),
        in_specs=[spec(operand.shape) for operand in operands],
        out_specs=[spec(shape) for shape in outs],
        out_shape=[jax.ShapeDtypeStruct(shape, jnp.float32) for shape in outs],
        compiler_params=pltpu.CompilerParams(vmem_limit_bytes=48 * 1024 * 1024),
    )(*operands)


def chained(through, local, reverse):
    order = range(local.shape[0])
    factor, running = (jnp.ones_like(through[0]), jnp.zeros_like(local[0]))
    factors, states = ([], [])
    for at in reversed(order) if reverse else order:
        factors.append(factor)
        states.append(running)
        factor, running = (factor * through[at], through[at] * running + local[at])
    if reverse:
        factors, states = (factors[::-1], states[::-1])
    return (factor, running, jnp.stack(factors), jnp.stack(states))


def summed_rows(value, groups):
    return lax.psum_scatter(value, groups, scatter_dimension=0, tiled=True)


def on_device(
    hidden_in,
    cotangent,
    positions,
    norm_gain,
    proj_z,
    proj_x,
    proj_bc,
    proj_dt,
    conv_inner,
    conv_inner_bias,
    conv_state,
    conv_state_bias,
    dt_bias,
    a_log,
    skip_gain,
    gated_gain,
    proj_out,
):
    row_count = hidden_in.shape[0]
    full_width = hidden_in.shape[1]
    tap_count = conv_inner.shape[0]
    rim_rows = tap_count - 1
    local_inner = proj_z.shape[1]
    local_heads = proj_dt.shape[1]
    head_width = local_inner // local_heads
    state_width = proj_bc.shape[1] // 2
    block_count = row_count // BLOCK
    groups = ("fsdp", "ctx")
    spare = jnp.zeros((proj_dt.shape[0], 128 - local_heads - 1), jnp.bfloat16)
    early = jnp.concatenate([proj_x, proj_bc, proj_dt, norm_gain[:, None], spare], axis=1)
    early = lax.all_gather(early, groups, axis=0, tiled=True)
    late = jnp.concatenate([proj_z, proj_out.T], axis=1)
    late = lax.all_gather(late, groups, axis=0, tiled=True)
    bc_end = local_inner + 2 * state_width
    weight_x, weight_bc = (early[:, :local_inner], early[:, local_inner:bc_end])
    weight_dt = early[:, bc_end : bc_end + local_heads]
    gain_full = early[:, bc_end + local_heads]
    weight_z, weight_out_t = (late[:, :local_inner], late[:, local_inner:])
    row_valid = (positions >= 0).astype(jnp.float32)
    starts = (positions == 0).astype(jnp.float32)
    hidden = hidden_in.astype(jnp.float32)
    row_scale = lax.rsqrt(jnp.mean(hidden * hidden, axis=1, keepdims=True) + EPS)
    normed = (hidden * row_scale * gain_full.astype(jnp.float32)[None, :]).astype(jnp.bfloat16)
    gate_z = jnp.dot(normed, weight_z, preferred_element_type=jnp.float32)
    inner_x = jnp.dot(normed, weight_x, preferred_element_type=jnp.float32)
    state_in = jnp.dot(normed, weight_bc, preferred_element_type=jnp.float32)
    step_raw = jnp.dot(normed, weight_dt, preferred_element_type=jnp.float32)
    rim_x, rim_bc = passed_along(
        (inner_x[row_count - rim_rows :], state_in[row_count - rim_rows :]), "ctx", 1
    )
    ext_x = jnp.concatenate([rim_x, inner_x], axis=0)
    ext_bc = jnp.concatenate([rim_bc, state_in], axis=0)
    pre_x = causal_conv(ext_x, conv_inner, conv_inner_bias, positions)
    pre_bc = causal_conv(ext_bc, conv_state, conv_state_bias, positions)
    conv_x = jax.nn.silu(pre_x)
    conv_bc = jax.nn.silu(pre_bc)
    state_b = conv_bc[:, :state_width]
    state_c = conv_bc[:, state_width:]
    shifted_step = step_raw + dt_bias[None, :]
    step_size = jax.nn.softplus(shifted_step)
    decay_rate = -jnp.exp(a_log)
    decay_log = step_size * decay_rate[None, :]
    inner_u = conv_x * jnp.repeat(step_size, head_width, axis=1)
    decay_blocks = decay_log.reshape(block_count, BLOCK, local_heads)
    start_blocks = starts.reshape(block_count, BLOCK)
    row_index = jnp.arange(BLOCK)
    lower = (row_index[:, None] >= row_index[None, :]).astype(jnp.float32)
    cumulative = jnp.einsum("ij,cjh->cih", lower, decay_blocks, precision=HIGHEST)
    segment = jnp.einsum("ij,cj->ci", lower, start_blocks, precision=HIGHEST)
    entry_decay = jnp.exp(cumulative) * (segment == 0).astype(jnp.float32)[:, :, None]
    closing = (segment == segment[:, -1:])[:, :, None]
    towards = jnp.where(closing, jnp.exp(cumulative[:, -1:] - cumulative), 0.0)
    through = entry_decay[:, -1]
    through_rows = jnp.repeat(through, head_width, axis=1)[:, :, None]
    cumulative_t = cumulative.transpose(0, 2, 1)
    seg_col, seg_row = (segment[:, :, None], segment[:, None, :])
    u_blocks = inner_u.reshape(block_count, BLOCK, local_inner)
    b_blocks = state_b.reshape(block_count, BLOCK, state_width)
    c_blocks = state_c.reshape(block_count, BLOCK, state_width)
    rows_shape = (block_count, BLOCK, local_inner)
    state_shape = (block_count, local_inner, state_width)
    side_shape = (block_count, BLOCK, state_width)
    make_state = functools.partial(state_kernel, head_width)
    (local_state,) = by_blocks(make_state, (towards, u_blocks, b_blocks), [state_shape], block_count)
    piece_decay, piece_state, prefix_decay, prefix_state = chained(
        through_rows, local_state, False
    )
    incoming = entering(piece_decay, piece_state, "ctx", False)
    block_in = prefix_decay * incoming[None] + prefix_state
    (scanned,) = by_blocks(
        functools.partial(scan_kernel, head_width),
        (
            cumulative,
            cumulative_t,
            seg_col,
            seg_row,
            entry_decay,
            u_blocks,
            b_blocks,
            c_blocks,
            block_in,
        ),
        [rows_shape],
        block_count,
    )
    skip_row = jnp.repeat(skip_gain, head_width)[None, :]
    mixed_out = scanned.reshape(row_count, local_inner) + skip_row * conv_x
    gate_act = jax.nn.silu(gate_z)
    gated_out = mixed_out * gate_act
    squares = pair_sum(jnp.sum(gated_out * gated_out, axis=1), "tp")
    gated_scale = lax.rsqrt(squares / INNER + EPS)[:, None]
    gnormed = (gated_out * gated_scale * gated_gain[None, :]).astype(jnp.bfloat16)
    partial_branch = contract_last(gnormed, weight_out_t)
    branch = pair_sum(partial_branch, "tp")
    hidden_out = (hidden + branch * row_valid[:, None]).astype(jnp.bfloat16)
    grad_branch = (cotangent.astype(jnp.float32) * row_valid[:, None]).astype(jnp.bfloat16)
    grad_wout_t = contract_rows(grad_branch, gnormed)
    grad_gnormed = jnp.dot(grad_branch, weight_out_t, preferred_element_type=jnp.float32)
    weighted = grad_gnormed * gated_gain[None, :]
    grad_ggain = jnp.sum(grad_gnormed * gated_out * gated_scale, axis=0)
    gated_dot = pair_sum(jnp.sum(weighted * gated_out, axis=1), "tp")[:, None]
    grad_gated = gated_scale * weighted - gated_out * gated_scale**3 * gated_dot / INNER
    grad_mixed = grad_gated * gate_act
    grad_z = (grad_gated * mixed_out * silu_grad(gate_z)).astype(jnp.bfloat16)
    grad_wz = contract_rows(normed, grad_z)
    grads_early = summed_rows(jnp.concatenate([grad_wout_t, grad_wz], axis=1), groups)
    grad_skip = jnp.sum((grad_mixed * conv_x).sum(axis=0).reshape(local_heads, head_width), axis=1)
    grad_y_blocks = grad_mixed.reshape(block_count, BLOCK, local_inner)
    (local_back,) = by_blocks(
        make_state, (entry_decay, grad_y_blocks, c_blocks), [state_shape], block_count
    )
    piece_factor, piece_back, suffix_decay, suffix_back = chained(through_rows, local_back, True)
    outgoing = entering(piece_decay, piece_back, "ctx", True)
    grad_out_blocks = suffix_decay * outgoing[None] + suffix_back
    head_rows = (block_count, BLOCK, local_heads)
    grad_u, grad_cum, grad_cum_t, grad_b, grad_c = by_blocks(
        functools.partial(back_kernel, head_width),
        (
            cumulative,
            cumulative_t,
            seg_col,
            seg_row,
            entry_decay,
            towards,
            u_blocks,
            grad_y_blocks,
            b_blocks,
            c_blocks,
            block_in,
            grad_out_blocks,
        ),
        [rows_shape, head_rows, (block_count, local_heads, BLOCK), side_shape, side_shape],
        block_count,
    )
    passed = (grad_out_blocks * block_in).reshape(block_count, local_heads, -1).sum(axis=2)
    grad_cum = grad_cum - grad_cum_t.transpose(0, 2, 1)
    grad_decay = jnp.einsum("ji,cjh->cih", lower, grad_cum, precision=HIGHEST)
    grad_decay = (grad_decay + (passed * through)[:, None, :]).reshape(row_count, local_heads)
    grad_u = grad_u.reshape(row_count, local_inner)
    step_rows = jnp.repeat(step_size, head_width, axis=1)
    grad_step = grad_decay * decay_rate[None, :] + jnp.sum(
        (grad_u * conv_x).reshape(row_count, local_heads, head_width), axis=2
    )
    grad_alog = jnp.sum(grad_decay * step_size, axis=0) * decay_rate
    grad_shift = grad_step * jax.nn.sigmoid(shifted_step)
    grad_dtbias = jnp.sum(grad_shift, axis=0)
    grad_raw = grad_shift.astype(jnp.bfloat16)
    grad_heads = grad_u * step_rows + skip_row * grad_mixed
    grad_pre_x = grad_heads * silu_grad(pre_x)
    grad_bc_part = jnp.concatenate(
        [grad_b.reshape(row_count, state_width), grad_c.reshape(row_count, state_width)], axis=1
    )
    grad_conv_bc = pair_sum(grad_bc_part, "tp")
    grad_pre_bc = grad_conv_bc * silu_grad(pre_bc)
    wgrad_x, bgrad_x, spread_x = conv_back(grad_pre_x, ext_x, conv_inner, positions)
    wgrad_bc, bgrad_bc, spread_bc = conv_back(grad_pre_bc, ext_bc, conv_state, positions)
    later_x, later_bc = passed_along((spread_x[:rim_rows], spread_bc[:rim_rows]), "ctx", -1)
    grad_inner_x = spread_x[rim_rows:].at[row_count - rim_rows :].add(later_x).astype(jnp.bfloat16)
    grad_state_in = (
        spread_bc[rim_rows:].at[row_count - rim_rows :].add(later_bc).astype(jnp.bfloat16)
    )
    first_tp = (lax.axis_index("tp") == 0).astype(jnp.float32)
    partial_grad = (
        contract_last(grad_z, weight_z)
        + contract_last(grad_inner_x, weight_x)
        + contract_last(grad_raw, weight_dt)
        + first_tp * contract_last(grad_state_in, weight_bc)
    )
    grad_normed = pair_sum(partial_grad, "tp")
    pulled = grad_normed * gain_full.astype(jnp.float32)[None, :]
    norm_dot = jnp.sum(pulled * hidden, axis=1, keepdims=True)
    grad_hidden = (
        row_scale * pulled
        - hidden * row_scale**3 * norm_dot / full_width
        + cotangent.astype(jnp.float32)
    )
    grad_gain = jnp.sum(grad_normed * hidden * row_scale, axis=0)
    grad_wx = contract_rows(normed, grad_inner_x)
    grad_wbc = contract_rows(normed, grad_state_in)
    grad_wdt = contract_rows(normed, grad_raw)
    filler = jnp.zeros((full_width, 128 - local_heads - 1), jnp.float32)
    grads_late = summed_rows(
        jnp.concatenate([grad_wx, grad_wbc, grad_wdt, grad_gain[:, None], filler], axis=1), groups
    )
    scattered = (
        grads_late[:, bc_end + local_heads],
        grads_early[:, local_inner:],
        grads_late[:, :local_inner],
        grads_late[:, local_inner:bc_end],
        grads_late[:, bc_end : bc_end + local_heads],
        grads_early[:, :local_inner].T,
    )
    small = (grad_ggain, wgrad_x, bgrad_x, wgrad_bc, bgrad_bc, grad_dtbias, grad_alog, grad_skip)
    flat = lax.psum(jnp.concatenate([part.reshape(-1) for part in small]), groups)
    reduced_small = []
    for part in small:
        reduced_small.append(flat[: part.size].reshape(part.shape))
        flat = flat[part.size :]
    return (
        hidden_out,
        grad_hidden,
        scattered[0],
        scattered[1],
        scattered[2],
        scattered[3],
        scattered[4],
        reduced_small[1],
        reduced_small[2],
        reduced_small[3],
        reduced_small[4],
        reduced_small[5],
        reduced_small[6],
        reduced_small[7],
        reduced_small[0],
        scattered[5],
    )


def solution(mesh):
    placed = (
        P(("fsdp", "ctx"), None),
        P(("fsdp", "ctx"), None),
        P(("fsdp", "ctx")),
        P(("fsdp", "ctx")),
        P(("fsdp", "ctx"), "tp"),
        P(("fsdp", "ctx"), "tp"),
        P(("fsdp", "ctx"), None),
        P(("fsdp", "ctx"), "tp"),
        P(None, "tp"),
        P("tp"),
        P(),
        P(),
        P("tp"),
        P("tp"),
        P("tp"),
        P("tp"),
        P("tp", ("fsdp", "ctx")),
    )
    return jax.shard_map(
        on_device,
        mesh=mesh,
        in_specs=placed,
        out_specs=(
            P(("fsdp", "ctx"), None),
            P(("fsdp", "ctx"), None),
            P(("fsdp", "ctx")),
            P(("fsdp", "ctx"), "tp"),
            P(("fsdp", "ctx"), "tp"),
            P(("fsdp", "ctx"), None),
            P(("fsdp", "ctx"), "tp"),
            P(None, "tp"),
            P("tp"),
            P(),
            P(),
            P("tp"),
            P("tp"),
            P("tp"),
            P("tp"),
            P("tp", ("fsdp", "ctx")),
        ),
        check_vma=False,
    )
```

time: 1980 us -> 692 us (0.35)
  waiting for transfers between devices: 618 us -> 122 us
  local copies, waits for them, and re-layouts: 435 us -> 95.6 us
  matrix products: 360 us -> 72.3 us
  other arithmetic: 294 us -> 153 us
  Pallas kernels: 0 us -> 132 us
  blocking collectives: 210 us -> 81 us
    reduce_scatter x4 -> x0, waiting for transfers between devices: 434 us -> none  [the longest x1 133 us: on_device(): lax.psum_scatter(grad_wz, ('fsdp', 'ctx'), scatter_dimension=0, tiled=True)]
    dot_general x99 -> x4, matrix products: 284 us -> 6.29 us  [the longest x1 5.6 us: on_device(): jnp.dot(grad_branch, weight_out_t, preferred_element_type=jnp.float32)]
    dynamic_update_slice x48 -> x0, local copies, waits for them, and re-layouts: 170 us -> none  [on_device(): lax.map(local_item, (decay_blocks, u_blocks, b_blocks, c_blocks, start_bl...]
    pallas_call x0 -> x4, Pallas kernels: none -> 132 us  [by_blocks(): pl.pallas_call(kernel, grid=(block_count,), in_specs=[spec(operand.shape)...]
    unnamed x3 -> x0, blocking collectives: 131 us -> none
    psum x2 -> x1, blocking collectives: 5.04 us -> 74.3 us  [on_device(): lax.psum(jnp.concatenate([part.reshape(-1) for part in small]), groups)]
    all_gather x2 -> x1, blocking collectives: 74.2 us -> 6.64 us  [entering(): decays, states = (lax.all_gather(decay, axis), lax.all_gather(state, axis))]
    scatter-add x14 -> x0, local copies, waits for them, and re-layouts: 50.8 us -> none  [the longest x6 49.8 us: conv_back(): spread.at[tap_count - 1 - offset:tap_count - 1 - offset + row_count]]
  transfers between devices with their start and end apart: 16 -> 15, of which waited for: 10 -> 5; matrix products, arithmetic and copies ran while one was open for 15% -> 36% of each run, Pallas kernels for 0% -> 16%
where the time goes in v1:
time: 692 us; the launch traced here: 685 us
  other arithmetic  153 us (22%)
  Pallas kernels  132 us (19%)
  waiting for transfers between devices  122 us (18%)
  local copies, waits for them, and re-layouts  95.6 us (14%)
  blocking collectives  81 us (12%)
  matrix products  72.3 us (10%)
  between operations  16.1 us (2%)
  starting transfers between devices  11.9 us (2%)
    pallas_call x4, Pallas kernels, by_blocks(): pl.pallas_call(kernel, grid=(block_count,), in_specs=[spec(operand.shape)...  132 us
    psum x1, blocking collectives, on_device(): lax.psum(jnp.concatenate([part.reshape(-1) for part in small]), groups)  74.3 us
    all_gather x1, waiting for transfers between devices, on_device(): early = lax.all_gather(early, groups, axis=0, tiled=True)  52 us
    unnamed x8, waiting for transfers between devices  39.4 us
    unnamed x237, local copies, waits for them, and re-layouts  37.7 us
    dot_general x5, matrix products, contract_last(): lax.dot_general(left, right, (((1,), (1,)), ((), ())), preferred_element_...  32.4 us
    reduce_sum x2, other arithmetic, conv_back(): weight_grads.append(jnp.sum(masked * window, axis=0))  29.3 us
    all_gather x1, waiting for transfers between devices, on_device(): late = lax.all_gather(late, groups, axis=0, tiled=True)  26.4 us
  transfers between devices with their start and end apart: 15, of which 5 were waited for; matrix products, arithmetic and copies ran while one was open for 36% of the time, Pallas kernels for 16%

profile of v1, /device:TPU:0, one launch (start us, length us, event | category | flops | bytes accessed | tf_op | source)
XLA Modules:
  0.0 684.6 jit_solution(736053683118776823)
XLA Ops:
  21.0 52.0 %all-gather.5.cloned.1.call-done = bf16[768,1152]{1,0:T(8,128)(2,1)} async-done(((bf16[48,1152]{1,0:T(8,128)(2,1)}), bf16[768,1152]{1,0:T(8,128)(2,1)}) %all-gather.5.cloned.1.call-update) | async-done | bytes 1769488 | tf_op jit(solution)/shard_map/all_gather | solution.py:279
  99.1 6.6 copy.81
  112.1 17.4 %fusion.72 = (f32[2048,768]{1,0:T(8,128)}, f32[2048,768]{1,0:T(8,128)}) fusion(f32[2048,768]{1,0:T(8,128)S(1)} %copy-done.17, f32[2048]{0:T(1024)S(1)} %copy-done.40, f32[2048,768]{1,0:T(8,128)} %copy-done.20, f32[3,768]{1,0:T(4,128)} %collective-permute-done, f32[768]{0:T(1024)S(1)} %copy-done.56, f32[2048]{0:T(1024)S(1)} %copy-done.42, ...), kind=kLoop, calls=%fused_computation.232 | loop fusion | flops 31457280 | bytes 25223168 | tf_op jit(solution)/shard_map/mul | solution.py:311
  129.5 12.2 %shard_map.288 = f32[8,768,128]{2,1,0:T(8,128)S(1)} custom-call(f32[8,256,12]{2,1,0:T(8,128)S(1)} %copy-done.12, f32[8,256,768]{2,1,0:T(8,128)} %bitcast.129, f32[8,256,128]{2,1,0:T(8,128)S(1)} %bitcast.122), custom_call_target="tpu_custom_call" | custom-call | tf_op jit(solution)/shard_map/pallas_call | solution.py:221
  156.1 6.6 all_gather.21
  178.7 33.6 %shard_map.289 = f32[8,256,768]{2,1,0:T(8,128)} custom-call(f32[8,256,12]{2,1,0:T(8,128)S(1)} %bitcast.117, f32[8,12,256]{2,1,0:T(8,128)S(1)} %fusion.60.cum_t_ref, f32[8,256,1]{2,1,0:T(8,128)S(1)} %copy-done.10, f32[8,1,256]{2,1,0:T(1,128)S(1)} %broadcast_in_dim.137.seg_t_ref, f32[8,256,12]{2,1,0:T(8,128)S(1)} %copy-done.1, f32[8,256,768]{2,1,0:T(8,128)} %bitcast.130, ...), custom_call_target="tpu_custom_call" | custom-call | tf_op jit(solution)/shard_map/pallas_call | solution.py:221
  212.3 26.4 %all-gather.9.cloned.1.call-done = bf16[768,1536]{1,0:T(8,128)(2,1)} async-done(((bf16[48,1536]{1,0:T(8,128)(2,1)}), bf16[768,1536]{1,0:T(8,128)(2,1)}) %all-gather.9.cloned.1.call-update) | async-done | bytes 2359312 | tf_op jit(solution)/shard_map/all_gather | solution.py:281
  238.7 9.7 %multiply_reduce_fusion.7 = (f32[2048]{0:T(1024)S(1)}, f32[2048,768]{1,0:T(8,128)S(1)}, f32[2048,768]{1,0:T(8,128)}) fusion(f32[2048,768]{1,0:T(8,128)} %get-tuple-element.169, f32[768]{0:T(1024)S(1)} %mul.1212, f32[8,256,768]{2,1,0:T(8,128)} %shard_map.289, bf16[2048,768]{1,0:T(8,128)(2,1)S(1)} %copy-done.14, ...), kind=kOutput, calls=%fused_computation.41 | convolution fusion | flops 2436364288 | bytes 29502464 | tf_op jit(solution)/shard_map/dot_general | solution.py:292
  249.9 5.6 multiply_reduce_fusion.5
  256.5 4.5 fusion.26
  261.0 15.4 %multiply_reduce_fusion = (f32[768]{0:T(1024)}, f32[2048,768]{1,0:T(8,128)}, bf16[2048,768]{1,0:T(8,128)(2,1)}) fusion(f32[2048,768]{1,0:T(8,128)S(1)} %bitcast.143, f32[2048,768]{1,0:T(8,128)} %get-tuple-element.224, f32[2048]{0:T(1024)S(1)} %add.369, f32[2048,768]{1,0:T(8,128)} %copy-done.25, f32[2048]{0:T(1024)S(1)} %get-tuple-element.154, ...), kind=kLoop, calls=%fused_computation.30 | loop fusion | flops 40893696 | bytes 40928256 | tf_op jit(solution)/shard_map/reduce_sum | solution.py:375
  276.5 12.2 %shard_map.290 = f32[8,768,128]{2,1,0:T(8,128)S(1)} custom-call(f32[8,256,12]{2,1,0:T(8,128)S(1)} %copy-done.2, f32[8,256,768]{2,1,0:T(8,128)} %bitcast.132, f32[8,256,128]{2,1,0:T(8,128)S(1)} %bitcast.121), custom_call_target="tpu_custom_call" | custom-call | tf_op jit(solution)/shard_map/pallas_call | solution.py:221
  290.8 5.8 fusion.81
  299.0 6.0 copy.95
  316.0 7.3 %fusion.34 = f32[2048,768]{1,0:T(8,128)} fusion(bf16[2048,768]{1,0:T(8,128)(2,1)} %get-tuple-element.170, bf16[768,1536]{1,0:T(8,128)(2,1)S(1)} %copy-done.89), kind=kOutput, calls=%fused_computation.90 | convolution fusion | flops 2415919104 | bytes 10616832 | tf_op jit(solution)/shard_map/dot_general | solution.py:47
  324.9 7.1 %multiply_reduce_fusion.8 = (f32[8,768]{1,0:T(8,128)}, f32[8,768,128]{2,1,0:T(8,128)}) fusion(f32[8,768,128]{2,1,0:T(8,128)} %broadcast_dynamic-update-slice_fusion, f32[768,128]{1,0:T(8,128)S(1)} %fusion.45, f32[8,768]{1,0:T(8,128)S(1)} %bitcast.158, f32[8,768,128]{2,1,0:T(8,128)} %constant_dynamic-update-slice_fusion.8, f32[768,128]{1,0:T(8,128)S(1)} %copy-done.29, ...), kind=kLoop, calls=%fused_computation.52 | loop fusion | flops 4712448 | bytes 10297344 | tf_op jit(solution)/shard_map/reduce_sum | solution.py:403
  332.0 74.2 %shard_map.291 = (f32[8,256,768]{2,1,0:T(8,128)}, f32[8,256,12]{2,1,0:T(8,128)S(1)}, f32[8,12,256]{2,1,0:T(8,128)S(1)}, f32[8,256,128]{2,1,0:T(8,128)S(1)}, f32[8,256,128]{2,1,0:T(8,128)S(1)}) custom-call(f32[8,256,12]{2,1,0:T(8,128)S(1)} %bitcast.118, f32[8,12,256]{2,1,0:T(8,128)S(1)} %fusion.60.cum_t_ref, f32[8,256,1]{2,1,0:T(8,128)S(1)} %copy-done.11, ...), custom_call_target="tpu_custom_call" | custom-call | tf_op jit(solution)/shard_map/pallas_call | solution.py:221
  408.3 24.2 %multiply_reduce_fusion.3 = (f32[768]{0:T(1024)S(1)}, f32[768]{0:T(1024)S(1)}, f32[768]{0:T(1024)S(1)}, f32[768]{0:T(1024)S(1)}, f32[768]{0:T(1024)S(1)}, /*index=5*/f32[2048,768]{1,0:T(8,128)S(1)}, f32[2048,768]{1,0:T(8,128)}) fusion(f32[2048]{0:T(1024)} %copy-done.38, f32[2048,768]{1,0:T(8,128)} %copy-done.20, f32[3,768]{1,0:T(4,128)} %collective-permute-done, ...), kind=kLoop, calls=%fused_computation.33 | loop fusion | flops 45609216 | bytes 44100608 | tf_op jit(solution)/shard_map/reduce_sum | solution.py:81
  432.6 9.6 %multiply_multiply_fusion.3 = (f32[2048,768]{1,0:T(8,128)}, f32[2048,768]{1,0:T(8,128)}, f32[2048,768]{1,0:T(8,128)}, f32[2048,768]{1,0:T(8,128)}) fusion(f32[2048,768]{1,0:T(8,128)S(1)} %get-tuple-element.141, f32[2048]{0:T(1024)S(1)} %get-tuple-element.213, f32[768]{0:T(1024)S(1)} %copy-done.53, f32[2048]{0:T(1024)S(1)} %copy-done.41, ...), kind=kLoop, calls=%fused_computation.50 | loop fusion | flops 12582912 | bytes 31502336 | tf_op jit(solution)/shard_map/mul | solution.py:83
  443.9 6.6 copy.88
  460.8 4.4 pad_add_fusion
  465.2 4.8 fusion.62
  473.8 7.6 %fusion.24 = f32[2048,768]{1,0:T(8,128)} fusion(bf16[2048,768]{1,0:T(8,128)(2,1)} %scatter-add.6, bf16[768,1152]{1,0:T(8,128)(2,1)} %all-gather.5.cloned.1.call-done), kind=kOutput, calls=%fused_computation.79 | convolution fusion | flops 2415919104 | bytes 10616832 | tf_op jit(solution)/shard_map/dot_general | solution.py:47
  481.5 5.0 multiply_reduce_fusion.11
  493.9 8.1 %multiply_add_fusion = f32[2048,768]{1,0:T(8,128)S(1)} fusion(f32[2048,768]{1,0:T(8,128)} %fusion.62, f32[2048,768]{1,0:T(8,128)} %fusion.34, f32[2048,768]{1,0:T(8,128)} %fusion.24, f32[]{:T(128)S(6)} %convert_element_type.107, bf16[2048,256]{1,0:T(8,128)(2,1)S(1)} %scatter-add.9, bf16[768,1152]{1,0:T(8,128)(2,1)} %all-gather.5.cloned.1.call-done), kind=kOutput, calls=%fused_computation.36 | convolution fusion | flops 811597824 | bytes 26607620 | tf_op jit(solution)/shard_map/dot_general | solution.py:47
  503.3 4.6 fusion.32
  509.8 4.2 fusion.82
  519.4 12.9 %concatenate.37 = f32[768,1152]{0,1:T(8,128)} concatenate(f32[768,768]{0,1:T(8,128)} %fusion.82, f32[768,256]{0,1:T(8,128)} %fusion.83, f32[768,12]{0,1:T(8,128)S(1)} %fusion.66, f32[768,1]{0,1:T(1,128)S(1)} %broadcast_in_dim.168, f32[768,115]{0,1:T(8,128)} %broadcast_in_dim.169), dimensions={1} | concatenate | bytes 7077888 | tf_op jit(solution)/shard_map/concatenate | solution.py:451
  532.3 5.2 copy.93
  538.6 74.3 %psum.7 = f32[5924]{0:T(1024)S(1)} all-reduce(f32[5924]{0:T(1024)S(1)} %concatenate.39), channel_id=1, replica_groups=mesh['fsdp'=4,'ctx'=4,'tp'=2] {'fsdp','ctx'}, use_global_device_ids=true, to_apply=%region_25.26 | all-reduce | flops 5924 | bytes 47392 | tf_op jit(solution)/shard_map/psum | solution.py:462
  617.6 14.6 %convert_add_fusion.1 = (f32[2048,768]{1,0:T(8,128)}, bf16[2048,768]{1,0:T(8,128)(2,1)}) fusion(bf16[2048,768]{1,0:T(8,128)(2,1)} %param.22, bf16[2048,768]{1,0:T(8,128)(2,1)S(1)} %copy-done.19, f32[2048]{0:T(1024)S(1)} %get-tuple-element.115, f32[2048]{0:T(1024)S(1)} %copy-done.64, f32[768]{0:T(1024)S(1)} %copy-done.51, f32[2048]{0:T(1024)S(1)} %copy-done.45, ...), kind=kLoop, calls=%fused_computation.8 | loop fusion | flops 22020096 | bytes 40930304 | tf_op jit(solution)/shard_map/add | solution.py:441
  632.2 39.3 %reduce-scatter.7.cloned.1.call-done = f32[48,1152]{1,0:T(8,128)} async-done(((f32[768,1152]{1,0:T(8,128)}), f32[48,1152]{1,0:T(8,128)}) %reduce-scatter.7.cloned.1.call-update) | async-done | bytes 221200
  (406 shorter events, 140.5 us)
Async XLA Ops:
  7.2 67.0 %copy-start.18 = (bf16[2048,768]{1,0:T(8,128)(2,1)S(1)}, bf16[2048,768]{1,0:T(8,128)(2,1)}, u32[]{:S(2)}) copy-start(bf16[2048,768]{1,0:T(8,128)(2,1)} %param.21) | copy-start | bytes 9437188
  7.2 65.9 %all-gather.5.cloned.1.call-start = ((), (), s32[]{:S(2)}) async-start(), calls=%async_computation.2 | async-start | bytes 1880064 | tf_op jit(solution)/shard_map/all_gather | solution.py:279
  10.6 162.4 %all-gather.7.cloned.1.call-start = ((), (), s32[]{:S(2)}) async-start(), calls=%async_computation.3 | async-start | bytes 1966080 | tf_op jit(solution)/shard_map/all_gather | solution.py:32
  11.9 100.1 %copy-start.38 = (f32[2048]{0:T(1024)}, f32[2048]{0:T(1024)S(1)}, u32[]{:S(2)}) copy-start(f32[2048]{0:T(1024)S(1)} %get-tuple-element.212) | copy-start | bytes 24580
  21.0 54.0 %copy-start.44 = (f32[2048]{0:T(1024)}, f32[2048]{0:T(1024)S(1)}, u32[]{:S(2)}) copy-start(f32[2048]{0:T(1024)S(1)} %get-tuple-element.208) | copy-start | bytes 24580
  79.1 33.0 %collective-permute-start = (f32[3,768]{1,0:T(4,128)}, f32[3,768]{1,0:T(4,128)}, u32[]{:S(2)}, u32[]{:S(2)}) collective-permute-start(f32[3,768]{1,0:T(4,128)} %slice.474), channel_id=1, source_target_pairs={{0,2},{2,4},{4,6},{1,3},{3,5},{5,7},{8,10},{10,12},{12,14},{9,11},... | collective-permute-start | bytes 27656 | tf_op jit(solution)/shard_map/ppermute | solution.py:21
  88.1 18.7 %copy-start.22 = (f32[2048,256]{1,0:T(8,128)}, f32[2048,256]{1,0:T(8,128)S(1)}, u32[]{:S(2)}) copy-start(f32[2048,256]{1,0:T(8,128)S(1)} %fusion.55) | copy-start | bytes 6291460
  88.7 18.0 %collective-permute-start.1 = (f32[3,256]{1,0:T(4,128)}, f32[3,256]{1,0:T(4,128)}, u32[]{:S(2)}, u32[]{:S(2)}) collective-permute-start(f32[3,256]{1,0:T(4,128)} %slice.480), channel_id=1, source_target_pairs={{0,2},{2,4},{4,6},{1,3},{3,5},{5,7},{8,10},{10,12},{12,14},{9,11},... | collective-permute-start | bytes 9224 | tf_op jit(solution)/shard_map/ppermute | solution.py:21
  105.9 35.9 %copy-start.63 = (f32[768]{0:T(1024)}, f32[768]{0:T(1024)S(1)}, u32[]{:S(2)}) copy-start(f32[768]{0:T(1024)S(1)} %broadcast_in_dim.157) | copy-start | bytes 9220
  143.9 94.8 %all-gather.9.cloned.1.call-start = ((), (), s32[]{:S(2)}) async-start(), calls=%async_computation.4 | async-start | bytes 2506752 | tf_op jit(solution)/shard_map/all_gather | solution.py:281
  145.6 177.7 %all-gather.11.cloned.1.call-start = ((), (), s32[]{:S(2)}) async-start(), calls=%async_computation.5 | async-start | bytes 1966080 | tf_op jit(solution)/shard_map/all_gather | solution.py:32
  145.8 115.2 %copy-start.60 = (f32[768]{0:T(1024)}, f32[768]{0:T(1024)S(1)}, u32[]{:S(2)}) copy-start(f32[768]{0:T(1024)S(1)} %mul.1212) | copy-start | bytes 9220
  148.3 20.6 %copy-start.31 = (f32[1,768,128]{2,1,0:T(8,128)S(1)}, f32[1,768,128]{2,1,0:T(8,128)}, u32[]{:S(2)}) copy-start(f32[1,768,128]{2,1,0:T(8,128)} %get-tuple-element.164) | copy-start | bytes 1179652
  148.3 21.5 %copy-start.30 = (f32[1,768,128]{2,1,0:T(8,128)S(1)}, f32[1,768,128]{2,1,0:T(8,128)}, u32[]{:S(2)}) copy-start(f32[1,768,128]{2,1,0:T(8,128)} %get-tuple-element.163) | copy-start | bytes 1179652
  178.7 60.0 %copy-start.14 = (bf16[2048,768]{1,0:T(8,128)(2,1)S(1)}, bf16[2048,768]{1,0:T(8,128)(2,1)}, u32[]{:S(2)}) copy-start(bf16[2048,768]{1,0:T(8,128)(2,1)} %copy-done.13) | copy-start | bytes 9437188
  248.4 1.4 collective-permute-start.2
  255.5 5.4 collective-permute-start.4
  290.7 325.2 %reduce-scatter.9.cloned.1.call-start = ((), (), s32[]{:S(2)}) async-start(), calls=%async_computation.7 | async-start | bytes 5013504
  315.0 356.5 %reduce-scatter.7.cloned.1.call-start = ((), (), s32[]{:S(2)}) async-start(), calls=%async_computation.6 | async-start | bytes 3760128
  408.2 24.3 %copy-start.39 = (f32[2048]{0:T(1024)S(1)}, f32[2048]{0:T(1024)}, u32[]{:S(2)}) copy-start(f32[2048]{0:T(1024)} %copy-done.38) | copy-start | bytes 24580
  408.2 24.3 %copy-start.41 = (f32[2048]{0:T(1024)S(1)}, f32[2048]{0:T(1024)}, u32[]{:S(2)}) copy-start(f32[2048]{0:T(1024)} %get-tuple-element.214) | copy-start | bytes 24580
  408.2 24.3 %copy-start.43 = (f32[2048]{0:T(1024)S(1)}, f32[2048]{0:T(1024)}, u32[]{:S(2)}) copy-start(f32[2048]{0:T(1024)} %get-tuple-element.215) | copy-start | bytes 24580
  408.2 24.3 %copy-start.53 = (f32[768]{0:T(1024)S(1)}, f32[768]{0:T(1024)}, u32[]{:S(2)}) copy-start(f32[768]{0:T(1024)} %get-tuple-element.132) | copy-start | bytes 9220
  408.2 24.3 %copy-start.55 = (f32[768]{0:T(1024)S(1)}, f32[768]{0:T(1024)}, u32[]{:S(2)}) copy-start(f32[768]{0:T(1024)} %get-tuple-element.133) | copy-start | bytes 9220
  408.2 24.3 %copy-start.57 = (f32[768]{0:T(1024)S(1)}, f32[768]{0:T(1024)}, u32[]{:S(2)}) copy-start(f32[768]{0:T(1024)} %get-tuple-element.134) | copy-start | bytes 9220
  408.2 24.3 %copy-start.59 = (f32[768]{0:T(1024)S(1)}, f32[768]{0:T(1024)}, u32[]{:S(2)}) copy-start(f32[768]{0:T(1024)} %get-tuple-element.135) | copy-start | bytes 9220
  443.6 37.9 %collective-permute-start.6 = (f32[2048,256]{1,0:T(8,128)}, f32[2048,256]{1,0:T(8,128)}, u32[]{:S(2)}, u32[]{:S(2)}) collective-permute-start(f32[2048,256]{1,0:T(8,128)} %pad_maximum_fusion.3), channel_id=1, source_target_pairs={{0,1},{1,0},{2,3},{3,2},{4,5},{5,4},{6,7},{7,6},{8,9},{9,8},{10,11... | collective-permute-start | bytes 6291464 | tf_op jit(solution)/shard_map/ppermute | solution.py:27
  455.1 17.3 %collective-permute-start.5 = (f32[3,768]{1,0:T(4,128)S(1)}, f32[3,768]{1,0:T(4,128)S(1)}, u32[]{:S(2)}, u32[]{:S(2)}) collective-permute-start(f32[3,768]{1,0:T(4,128)S(1)} %pad_add_fusion.2), channel_id=1, source_target_pairs={{2,0},{4,2},{6,4},{3,1},{5,3},{7,5},{10,8},{12,10},{14,12},{11,9},... | collective-permute-start | bytes 27656 | tf_op jit(solution)/shard_map/ppermute | solution.py:21
  488.2 5.5 collective-permute-start.7
  502.0 14.0 %collective-permute-start.8 = (f32[2048,768]{1,0:T(8,128)S(1)}, f32[2048,768]{1,0:T(8,128)S(1)}, u32[]{:S(2)}, u32[]{:S(2)}) collective-permute-start(f32[2048,768]{1,0:T(8,128)S(1)} %multiply_add_fusion), channel_id=1, source_target_pairs={{0,1},{1,0},{2,3},{3,2},{4,5},{5,4},{6,7},{7,6},{8,9},{9,8},{10,11... | collective-permute-start | bytes 18874376 | tf_op jit(solution)/shard_map/ppermute | solution.py:27
  507.9 109.7 %collective-permute-start.3 = (f32[2048,768]{1,0:T(8,128)}, f32[2048,768]{1,0:T(8,128)}, u32[]{:S(2)}, u32[]{:S(2)}) collective-permute-start(f32[2048,768]{1,0:T(8,128)} %fusion.32), channel_id=1, source_target_pairs={{0,1},{1,0},{2,3},{3,2},{4,5},{5,4},{6,7},{7,6},{8,9},{9,8},{10,11... | collective-permute-start | bytes 18874376 | tf_op jit(solution)/shard_map/ppermute | solution.py:27
  537.5 80.1 %copy-start.64 = (f32[2048]{0:T(1024)S(1)}, f32[2048]{0:T(1024)}, u32[]{:S(2)}) copy-start(f32[2048]{0:T(1024)} %get-tuple-element.207) | copy-start | bytes 24580
  (89 other events, 561.7 us)
Sparse Core Ops, SparseCore 0:
  11.4 61.6 all-gather.4
  144.0 28.8 all-gather.6
  176.3 62.3 all-gather.8
  290.8 29.7 all-gather.10
  325.7 137.3 reduce-scatter.8
  537.6 133.8 reduce-scatter.6
